TPU v7x, 32 devices: a whole 2x2x4 slice. The times are simulated.
32 devices in a mesh: dom: 2 (over y), dp: 16 (over z, x, core).
Axes of the slice: x: 2, y: 2, z: 4, core: 2. Of those that a mesh axis runs over, the one named last changes fastest.
Arguments:
- positions: float32 [128, 32768], P('dom', 'dp'), may hold values from -6 to 6
- ancestors: int32 [128], P('dom'), may hold values from 0 to 127
- block_choice: int32 [16, 16], replicated, may hold values from 0 to 15
- tile_slot: int32 [256, 8], P('dp'), may hold values from 0 to 15, all different within a row
- design: bfloat16 [32768, 1024], P('dp'), may hold values from -0.1875 to 0.1875
- labels: int32 [32768], P('dp'), may hold values 0 or 1
- row_section: int32 [32768], P('dp'), may hold values from 0 to 4
Outputs:
- advanced: float32 [128, 32768], P('dom', 'dp')
- mean_loglik: float32 [128], P('dom')
Inputs may be any that keep to these rules, and one draw needn't show every extreme that they name: Each row of tile_slot names 8 different owners.
All inputs are finite; a program needn't handle non-finite values. No bound on the sum of `labels` on one device may be relied on, other than what follows from the above.
Results may differ from a plain program's by a relative error of at most 0.00048.
Values may be sent and summed in bfloat16 or wider, within the bound.
A program may use at most 64 MiB of HBM per device.

v0:
```python
import jax
import jax.numpy as jnp
from jax import lax
from jax.sharding import PartitionSpec as P

TILE = 128
CURRENT = 2


step_size = 1.0
prior_precision = 0.05


def spread_blocks(source, block_choice, device_index):
    narrow = source.astype(jnp.bfloat16)
    particle_count = narrow.shape[0]
    blocks_owned = narrow.shape[1] // TILE
    wanted = lax.dynamic_index_in_dim(block_choice, device_index, 1, keepdims=False)
    blocks = narrow.reshape(particle_count, blocks_owned, TILE)
    outgoing = jnp.take(blocks, wanted, axis=1)
    return lax.all_to_all(outgoing, "dp", split_axis=1, concat_axis=1, tiled=True)


def tile_logits(fetched, design_tiles, tile_slot):
    weights = jnp.take(fetched, tile_slot, axis=1)
    return jnp.einsum("bikc,pbkc->bpi", design_tiles, weights, preferred_element_type=jnp.float32)


def shards(positions, ancestors, block_choice, tile_slot, design, labels, row_section):
    data_width = lax.axis_size("dp")
    device_index = lax.axis_index("dp")
    lineage = lax.all_gather(positions, "dom", axis=0, tiled=True)
    resampled = jnp.take(lineage, ancestors, axis=0)
    particle_count = resampled.shape[0]
    blocks_owned = positions.shape[1] // TILE
    blocks_dev = tile_slot.shape[0]
    per_block = tile_slot.shape[1]
    design_tiles = design.reshape(blocks_dev, TILE, per_block, TILE)
    targets = labels.reshape(blocks_dev, 1, TILE).astype(jnp.float32)
    sections = row_section.reshape(blocks_dev, 1, TILE)
    fetched = spread_blocks(resampled, block_choice, device_index)
    logits = tile_logits(fetched, design_tiles, tile_slot)
    residual = jnp.where(sections <= CURRENT, targets - jax.nn.sigmoid(logits), 0.0).astype(
        jnp.bfloat16
    )
    per_tile = jnp.einsum(
        "bpi,bikc->bkpc", residual, design_tiles, preferred_element_type=jnp.float32
    )
    flat_terms = per_tile.reshape(blocks_dev * per_block, particle_count * TILE)
    outgoing = jax.ops.segment_sum(flat_terms, tile_slot.reshape(-1), num_segments=data_width)
    outgoing = outgoing.reshape(data_width, particle_count, TILE)
    incoming = lax.all_to_all(outgoing, "dp", split_axis=0, concat_axis=0, tiled=True)
    column = lax.dynamic_index_in_dim(block_choice, device_index, 1, keepdims=False)
    owner_hot = (column[:, None] == jnp.arange(blocks_owned)[None, :]).astype(jnp.float32)
    gradient = jnp.einsum("spc,sq->pqc", incoming, owner_hot, precision=lax.Precision.HIGHEST)
    gradient = gradient.reshape(particle_count, blocks_owned * TILE)
    advanced = resampled + step_size * (gradient - prior_precision * resampled)
    fetched_new = spread_blocks(advanced, block_choice, device_index)
    logits_new = tile_logits(fetched_new, design_tiles, tile_slot)
    chosen = sections == CURRENT + 1
    loglik = jnp.where(chosen, targets * logits_new - jax.nn.softplus(logits_new), 0.0)
    totals = jnp.sum(loglik, axis=(0, 2))
    counted = jnp.sum(chosen.astype(jnp.float32))
    totals, counted = lax.psum((totals, counted), "dp")
    return (advanced, totals / jnp.maximum(counted, 1.0))


def solution(mesh):
    return jax.shard_map(
        shards,
        mesh=mesh,
        in_specs=(P("dom", "dp"), P("dom"), P(), P("dp", None), P("dp", None), P("dp"), P("dp")),
        out_specs=(P("dom", "dp"), P("dom")),
        check_vma=False,
    )
```

profile of v0, /device:TPU:0, one launch (start us, length us, event | category | flops | bytes accessed | tf_op | source)
XLA Modules:
  0.0 149.6 jit_solution(16209067632957137672)
XLA Ops:
  7.2 0.7 all-gather.2.cloned.1.call-update
  8.1 0.7 compare_select_fusion.1
  9.0 0.7 compare_select_fusion.3
  9.6 0.7 compare_and_fusion.2
  10.3 0.7 compare_and_fusion
  11.0 22.6 %all-gather.2.cloned.1.call-done = f32[128,2048]{1,0:T(8,128)} async-done(((f32[64,2048]{1,0:T(8,128)}), f32[128,2048]{1,0:T(8,128)}) %all-gather.2.cloned.1.call-update) | async-done | bytes 1048592 | tf_op jit(solution)/shard_map/all_gather | solution.py:32
  33.6 2.2 %gather_fusion = f32[64,2048]{1,0:T(8,128)S(1)} fusion(f32[128,2048]{1,0:T(8,128)} %all-gather.2.cloned.1.call-done, s32[1024]{0:T(1024)S(1)} %pad_clamp_fusion.2), kind=kCustom, calls=%fused_computation.4 | custom fusion | bytes 1048832 | tf_op jit(solution)/shard_map/jit(_take)/gather | solution.py:33
  36.7 0.8 select_bitcast_fusion.1
  37.5 5.6 %all-to-all-start = ((bf16[64,16,128]{2,0,1:T(8,128)(2,1)}), bf16[64,16,128]{2,0,1:T(8,128)(2,1)S(1)}, u32[]{:S(2)}, u32[]{:S(2)}) async-start(bf16[64,16,128]{2,0,1:T(8,128)(2,1)} %select_bitcast_fusion.1), calls=%async_computation | async-start | bytes 524288 | tf_op jit(solution)/shard_map/all_to_all | solution.py:21
  43.3 5.2 %copy.42 = bf16[256,8,8,128]{3,2,1,0:T(8,128)(2,1)} copy(bf16[256,8,8,128]{3,1,2,0:T(8,128)(2,1)} %bitcast.109) | data formatting | bytes 8388608
  48.7 4.5 %all-to-all-done = bf16[64,16,128]{2,0,1:T(8,128)(2,1)S(1)} async-done(((bf16[64,16,128]{2,0,1:T(8,128)(2,1)}), bf16[64,16,128]{2,0,1:T(8,128)(2,1)S(1)}, u32[]{:S(2)}, u32[]{:S(2)}) %all-to-all-start) | async-done | bytes 262176 | tf_op jit(solution)/shard_map/all_to_all | solution.py:21
  53.2 0.9 gather_fusion.2
  54.2 7.6 %fusion.9 = f32[16,8,64,128]{3,2,1,0:T(8,128)} fusion(bf16[16,128,8,128]{3,2,1,0:T(8,128)(2,1)} %bitcast.110, bf16[16,8,64,128]{3,2,1,0:T(8,128)(2,1)S(1)} %bitcast.115, pred[16,8]{1,0:T(8,128)(4,1)S(1)} %copy.28, f32[16,128]{1,0:T(8,128)S(1)} %convert_bitcast_fusion, pred[16,128]{1,0:T(8,128)(4,1)S(1)} %compare_bitcast_fusion), kind=kOutput, calls=%fused_computation.15 | convolution fusion | flops 538705920 | bytes 10496128 | tf_op jit(solution)/shard_map/bpi,bikc->bkpc/dot_general | solution.py:46
  61.8 9.6 %scatter_custom_fusion = f32[16,8192]{1,0:T(8,128)S(1)} fusion(s32[128]{0:T(128)S(1)} %reshape.119, f32[16,8,64,128]{3,2,1,0:T(8,128)} %fusion.9, f32[]{:T(128)} %constant.42.clone.1), kind=kCustom, calls=%fused_computation.6 | custom fusion | flops 1048576 | bytes 4718596 | tf_op jit(solution)/shard_map/scatter-add | solution.py:50
  71.6 17.2 %all_to_all.15 = f32[16,64,128]{2,1,0:T(8,128)S(1)} all-to-all(f32[16,64,128]{2,1,0:T(8,128)S(1)} %bitcast.116), channel_id=1, replica_groups=mesh['dom'=2,'dp'=16] {'dp'}, dimensions={0} | all-to-all | bytes 1048576 | tf_op jit(solution)/shard_map/all_to_all | solution.py:52
  88.8 0.7 fusion.80
  90.2 0.8 select_bitcast_fusion
  91.0 4.1 %all-to-all-start.2 = ((bf16[64,16,128]{2,0,1:T(8,128)(2,1)}), bf16[64,16,128]{2,0,1:T(8,128)(2,1)S(1)}, u32[]{:S(2)}, u32[]{:S(2)}) async-start(bf16[64,16,128]{2,0,1:T(8,128)(2,1)} %select_bitcast_fusion), calls=%async_computation.2 | async-start | bytes 524288 | tf_op jit(solution)/shard_map/all_to_all | solution.py:21
  95.1 0.6 convert_reduce_fusion
  95.7 1.0 fusion.78
  96.7 8.4 %all-to-all-done.2 = bf16[64,16,128]{2,0,1:T(8,128)(2,1)S(1)} async-done(((bf16[64,16,128]{2,0,1:T(8,128)(2,1)}), bf16[64,16,128]{2,0,1:T(8,128)(2,1)S(1)}, u32[]{:S(2)}, u32[]{:S(2)}) %all-to-all-start.2) | async-done | bytes 262176 | tf_op jit(solution)/shard_map/all_to_all | solution.py:21
  105.1 0.9 gather_fusion.4
  106.1 3.9 %fusion.77 = f32[64]{0:T(128)S(1)} fusion(bf16[16,128,8,128]{3,2,1,0:T(8,128)(2,1)} %bitcast.111, bf16[16,8,64,128]{3,2,1,0:T(8,128)(2,1)S(1)} %bitcast.114, pred[16,8]{1,0:T(8,128)(4,1)S(1)} %copy.28, f32[16,128]{1,0:T(8,128)S(1)} %convert_bitcast_fusion, pred[16,128]{1,0:T(8,128)(4,1)S(1)} %bitcast.117), kind=kOutput, calls=%fused_computation.37 | convolution fusion | flops 270794688 | bytes 6302080 | tf_op jit(solution)/shard_map/bikc,pbkc->bpi/dot_general | solution.py:26
  110.0 31.5 %all-reduce = (f32[64]{0:T(128)S(1)}, f32[]{:T(128)}) all-reduce(f32[64]{0:T(128)S(1)} %fusion.77, f32[]{:T(128)} %get-tuple-element.6), channel_id=1, replica_groups=mesh['dom'=2,'dp'=16] {'dp'}, use_global_device_ids=true, to_apply=%region_2.5 | all-reduce | flops 65 | bytes 520 | tf_op jit(solution)/shard_map/psum | solution.py:64
  (30 shorter events, 2.9 us)
Async XLA Ops:
  7.2 0.8 copy-start
  7.2 26.4 %all-gather.2.cloned.1.call-start = ((), (), s32[]{:S(2)}) async-start(), calls=%async_computation.3 | async-start | bytes 1572864 | tf_op jit(solution)/shard_map/all_gather | solution.py:32
  11.0 32.2 %copy-start.1 = (s32[16,8]{0,1:T(8,128)S(1)}, s32[16,8]{0,1:T(8,128)}, u32[]{:S(2)}) copy-start(s32[16,8]{0,1:T(8,128)} %param.14) | copy-start | bytes 1540
  37.5 15.7 %all-to-all-start = ((bf16[64,16,128]{2,0,1:T(8,128)(2,1)}), bf16[64,16,128]{2,0,1:T(8,128)(2,1)S(1)}, u32[]{:S(2)}, u32[]{:S(2)}) async-start(bf16[64,16,128]{2,0,1:T(8,128)(2,1)} %select_bitcast_fusion.1), calls=%async_computation | async-start | bytes 524288 | tf_op jit(solution)/shard_map/all_to_all | solution.py:21
  43.3 5.4 %copy-start.2 = (s32[2048]{0:T(1024)S(1)}, s32[2048]{0:T(1024)}, u32[]{:S(2)}) copy-start(s32[2048]{0:T(1024)} %param.17) | copy-start | bytes 24580
  43.3 5.4 %copy-start.3 = (s32[2048]{0:T(1024)S(1)}, s32[2048]{0:T(1024)}, u32[]{:S(2)}) copy-start(s32[2048]{0:T(1024)} %param.16) | copy-start | bytes 24580
  91.0 14.1 %all-to-all-start.2 = ((bf16[64,16,128]{2,0,1:T(8,128)(2,1)}), bf16[64,16,128]{2,0,1:T(8,128)(2,1)S(1)}, u32[]{:S(2)}, u32[]{:S(2)}) async-start(bf16[64,16,128]{2,0,1:T(8,128)(2,1)} %select_bitcast_fusion), calls=%async_computation.2 | async-start | bytes 524288 | tf_op jit(solution)/shard_map/all_to_all | solution.py:21
Sparse Core Ops, SparseCore 0:
  9.6 23.9 all-gather.1
where the time goes:
time: 150 us
  blocking collectives  48.7 us (32%)
  waiting for transfers between devices  36.2 us (24%)
  other arithmetic  16.3 us (11%)
  between operations  14.9 us (10%)
  matrix products  12.3 us (8%)
  local copies, waits for them, and re-layouts  11.5 us (8%)
  starting transfers between devices  9.73 us (6%)
    psum x1, blocking collectives, shards(): totals, counted = lax.psum((totals, counted), 'dp')  31.5 us
    all_gather x1, waiting for transfers between devices, shards(): lineage = lax.all_gather(positions, 'dom', axis=0, tiled=True)  22.6 us
    all_to_all x1, blocking collectives, shards(): lax.all_to_all(outgoing, 'dp', split_axis=0, concat_axis=0, tiled=True)  17.2 us
    all_to_all x2, waiting for transfers between devices, spread_blocks(): lax.all_to_all(outgoing, 'dp', split_axis=1, concat_axis=1, tiled=True)  12.9 us
    all_to_all x2, starting transfers between devices, spread_blocks(): lax.all_to_all(outgoing, 'dp', split_axis=1, concat_axis=1, tiled=True)  9.7 us
    scatter-add x1, other arithmetic, shards(): jax.ops.segment_sum(flat_terms, tile_slot.reshape(-1), num_segments=data_...  9.64 us
    dot_general x1, matrix products, shards(): jnp.einsum('bpi,bikc->bkpc', residual, design_tiles, preferred_element_ty...  7.63 us
    unnamed x12, local copies, waits for them, and re-layouts  5.52 us
  transfers between devices with their start and end apart: 3, of which 3 were waited for; matrix products, arithmetic and copies ran while one was open for 7% of the time, Pallas kernels for 0%

commit v1 on v0

v1 whole, which is shorter than its diff:
```python
import functools

import jax
import jax.numpy as jnp
from jax import lax
from jax.experimental import pallas as pl
from jax.experimental.pallas import tpu as pltpu
from jax.sharding import PartitionSpec as P

TILE = 128
CURRENT = 2
STEP_SIZE = 1.0
PRIOR_PRECISION = 0.05
MESH = pl.DeviceIdType.MESH
F32, BF16 = jnp.float32, jnp.bfloat16


def round_kernel(
    groups,
    width,
    choice,
    slots,
    inverse,
    positions,
    ancestors,
    design_hbm,
    labels,
    sections,
    advanced,
    mean_out,
    design,
    narrow,
    picked,
    picked_all,
    lineage,
    resampled,
    outgoing,
    fetched,
    terms,
    sums,
    incoming,
    outgoing_new,
    fetched_new,
    totals_own,
    totals_all,
    design_sem,
    dom_send,
    dom_recv,
    pos_send,
    pos_recv,
    out_send,
    out_recv,
    grad_send,
    grad_recv,
    new_send,
    new_recv,
    tot_send,
    tot_recv,
):
    me, group = lax.axis_index("dp"), lax.axis_index("dom")
    particles = positions.shape[0]
    blocks_owned = positions.shape[1] // TILE
    blocks_dev, per_block = slots.shape

    def to_dp(source, target, sends, receives, device):
        return pltpu.make_async_remote_copy(
            src_ref=source,
            dst_ref=target.at[me],
            send_sem=sends.at[device],
            recv_sem=receives.at[me],
            device_id=(group, device),
            device_id_type=MESH,
        )

    def from_dp(source, target, sends, receives, device):
        return pltpu.make_async_remote_copy(
            src_ref=source,
            dst_ref=target.at[device],
            send_sem=sends.at[device],
            recv_sem=receives.at[device],
            device_id=(group, device),
            device_id_type=MESH,
        )

    def others(body):
        def step(offset, carry):
            body(lax.rem(me + offset, width))
            return carry

        lax.fori_loop(1, width, step, 0)

    barrier = pltpu.get_barrier_semaphore()

    def greet(device):
        pl.semaphore_signal(barrier, inc=1, device_id=(group, device), device_id_type=MESH)

    others(greet)
    for offset in range(1, groups):
        pl.semaphore_signal(
            barrier, inc=1, device_id=(lax.rem(group + offset, groups), me), device_id_type=MESH
        )
    design_copy = pltpu.make_async_copy(design_hbm, design, design_sem)
    design_copy.start()

    for block in range(blocks_owned):
        narrow[block] = positions[:, block * TILE : (block + 1) * TILE].astype(BF16)

    def pick(device, carry):
        value = narrow[choice[device, me]]
        picked[device] = value
        picked_all[group, device] = value
        return carry

    lax.fori_loop(0, width, pick, 0)
    origin = lax.broadcasted_iota(jnp.int32, (groups * particles, particles), 0)
    hot = (origin == ancestors[...]).astype(F32).T.astype(BF16)
    pl.semaphore_wait(barrier, width + groups - 2)

    def dom_copy(device, offset, incoming_side):
        sign = groups - offset if incoming_side else offset
        peer = lax.rem(group + sign, groups)
        return pltpu.make_async_remote_copy(
            src_ref=picked.at[device],
            dst_ref=picked_all.at[peer if incoming_side else group, device],
            send_sem=dom_send.at[offset - 1, device],
            recv_sem=dom_recv.at[offset - 1, device],
            device_id=(peer, me),
            device_id_type=MESH,
        )

    def position_copy(offset, incoming_side):
        sign = groups - offset if incoming_side else offset
        peer = lax.rem(group + sign, groups)
        return pltpu.make_async_remote_copy(
            src_ref=positions,
            dst_ref=lineage.at[peer if incoming_side else group],
            send_sem=pos_send.at[offset - 1],
            recv_sem=pos_recv.at[offset - 1],
            device_id=(peer, me),
            device_id_type=MESH,
        )

    def send_picked(device):
        for offset in range(1, groups):
            dom_copy(device, offset, False).start()

    others(send_picked)
    send_picked(me)
    for offset in range(1, groups):
        position_copy(offset, False).start()

    def resample(device):
        for offset in range(1, groups):
            dom_copy(device, offset, True).wait_recv()
        rows = picked_all[:, device].reshape(groups * particles, TILE)
        return jnp.dot(hot, rows, preferred_element_type=F32).astype(BF16)

    def send_resampled(device):
        outgoing[device] = resample(device)
        to_dp(outgoing.at[device], fetched, out_send, out_recv, device).start()

    others(send_resampled)
    fetched[me] = resample(me)
    terms[blocks_dev * per_block] = jnp.zeros((particles, TILE), F32)
    design_copy.wait()
    others(lambda device: from_dp(outgoing.at[device], fetched, out_send, out_recv, device).wait_recv())

    def logits_of(source, row_block):
        weights = jnp.concatenate(
            [source[slots[row_block, place]] for place in range(per_block)], axis=1
        )
        tiles = design[pl.ds(pl.multiple_of(row_block * TILE, TILE), TILE), :]
        logits = lax.dot_general(
            weights, tiles, (((1,), (1,)), ((), ())), preferred_element_type=F32
        )
        target = labels[pl.ds(row_block, 1), :].astype(F32)
        section = sections[pl.ds(row_block, 1), :]
        return tiles, logits, target, section

    def gradient_terms(row_block, carry):
        tiles, logits, target, section = logits_of(fetched, row_block)
        residual = jnp.where(section <= CURRENT, target - jax.nn.sigmoid(logits), 0.0).astype(BF16)
        product = jnp.dot(residual, tiles, preferred_element_type=F32)
        for place in range(per_block):
            terms[row_block * per_block + place] = product[:, place * TILE : (place + 1) * TILE]
        return carry

    lax.fori_loop(0, blocks_dev, gradient_terms, 0, unroll=4)

    def summed(device):
        total = terms[inverse[device, 0]]
        for row_block in range(1, blocks_dev):
            total = total + terms[inverse[device, row_block]]
        return total

    def send_sum(device):
        sums[device] = summed(device)
        to_dp(sums.at[device], incoming, grad_send, grad_recv, device).start()

    others(send_sum)
    incoming[me] = summed(me)

    lineage[group] = positions[...]
    for offset in range(1, groups):
        position_copy(offset, True).wait_recv()
    for block in range(blocks_owned):
        span = slice(block * TILE, (block + 1) * TILE)
        rows = lineage[:, :, span].reshape(groups * particles, TILE)
        high = rows.astype(BF16)
        low = (rows - high.astype(F32)).astype(BF16)
        resampled[block] = jnp.dot(hot, high, preferred_element_type=F32) + jnp.dot(
            hot, low, preferred_element_type=F32
        )

    others(lambda device: from_dp(sums.at[device], incoming, grad_send, grad_recv, device).wait_recv())
    for block in range(blocks_owned):
        gradient = jnp.zeros((particles, TILE), F32)
        for device in range(width):
            mine = (choice[device, me] == block).astype(F32)
            gradient = gradient + mine * incoming[device]
        kept = resampled[block]
        moved = kept + STEP_SIZE * (gradient - PRIOR_PRECISION * kept)
        advanced[:, block * TILE : (block + 1) * TILE] = moved
        narrow[block] = moved.astype(BF16)

    def send_new(device):
        outgoing_new[device] = narrow[choice[device, me]]
        to_dp(outgoing_new.at[device], fetched_new, new_send, new_recv, device).start()

    others(send_new)
    fetched_new[me] = narrow[choice[me, me]]
    others(
        lambda device: from_dp(
            outgoing_new.at[device], fetched_new, new_send, new_recv, device
        ).wait_recv()
    )

    def likelihood(row_block, carry):
        total, counted = carry
        _, logits, target, section = logits_of(fetched_new, row_block)
        chosen = section == CURRENT + 1
        softplus = jnp.maximum(logits, 0.0) + jnp.log(1.0 + jnp.exp(-jnp.abs(logits)))
        return (
            total + jnp.where(chosen, target * logits - softplus, 0.0),
            counted + chosen.astype(F32),
        )

    total, counted = lax.fori_loop(
        0,
        blocks_dev,
        likelihood,
        (jnp.zeros((particles, TILE), F32), jnp.zeros((1, TILE), F32)),
        unroll=4,
    )
    both = jnp.concatenate([total, jnp.broadcast_to(counted, (particles, TILE))], axis=0)
    row = jnp.sum(both.T, axis=0, keepdims=True)
    row = jnp.broadcast_to(row, totals_own.shape)
    totals_own[...] = row
    totals_all[me] = row
    others(lambda device: to_dp(totals_own, totals_all, tot_send, tot_recv, device).start())
    others(lambda device: from_dp(totals_own, totals_all, tot_send, tot_recv, device).wait_recv())
    final = jnp.sum(totals_all[...], axis=0)
    mean_out[...] = final[:1, :particles] / jnp.maximum(final[:1, particles:], 1.0)

    def wait_sends(device):
        to_dp(outgoing.at[device], fetched, out_send, out_recv, device).wait_send()
        to_dp(sums.at[device], incoming, grad_send, grad_recv, device).wait_send()
        to_dp(outgoing_new.at[device], fetched_new, new_send, new_recv, device).wait_send()
        to_dp(totals_own, totals_all, tot_send, tot_recv, device).wait_send()

    others(wait_sends)

    def wait_dom(device, carry):
        for offset in range(1, groups):
            dom_copy(device, offset, False).wait_send()
        return carry

    lax.fori_loop(0, width, wait_dom, 0)
    for offset in range(1, groups):
        position_copy(offset, False).wait_send()


def shards(positions, ancestors, block_choice, tile_slot, design, labels, row_section):
    width, groups = lax.axis_size("dp"), lax.axis_size("dom")
    particles, features = positions.shape
    blocks_owned = features // TILE
    blocks_dev, per_block = tile_slot.shape
    tiles = blocks_dev * per_block
    numbers = jnp.arange(tiles, dtype=jnp.int32).reshape(1, blocks_dev, per_block)
    owners = jnp.arange(width, dtype=jnp.int32)[:, None, None]
    inverse = jnp.min(jnp.where(tile_slot[None] == owners, numbers, tiles), axis=2)

    smem = pl.BlockSpec(memory_space=pltpu.SMEM)
    vmem = pl.BlockSpec(memory_space=pltpu.VMEM)
    block = (particles, TILE)
    dma = pltpu.SemaphoreType.DMA
    advanced, mean = pl.pallas_call(
        functools.partial(round_kernel, groups, width),
        out_shape=(
            jax.ShapeDtypeStruct((particles, features), F32),
            jax.ShapeDtypeStruct((1, particles), F32),
        ),
        in_specs=[smem, smem, smem, vmem, vmem, pl.BlockSpec(memory_space=pl.ANY), vmem, vmem],
        out_specs=(vmem, vmem),
        scratch_shapes=[
            pltpu.VMEM(design.shape, BF16),
            pltpu.VMEM((blocks_owned, *block), BF16),
            pltpu.VMEM((width, *block), BF16),
            pltpu.VMEM((groups, width, *block), BF16),
            pltpu.VMEM((groups, particles, features), F32),
            pltpu.VMEM((blocks_owned, *block), F32),
            pltpu.VMEM((width, *block), BF16),
            pltpu.VMEM((width, *block), BF16),
            pltpu.VMEM((tiles + 1, *block), F32),
            pltpu.VMEM((width, *block), F32),
            pltpu.VMEM((width, *block), F32),
            pltpu.VMEM((width, *block), BF16),
            pltpu.VMEM((width, *block), BF16),
            pltpu.VMEM((8, 2 * particles), F32),
            pltpu.VMEM((width, 8, 2 * particles), F32),
            dma,
            dma((max(groups - 1, 1), width)),
            dma((max(groups - 1, 1), width)),
            dma((max(groups - 1, 1),)),
            dma((max(groups - 1, 1),)),
            dma((width,)),
            dma((width,)),
            dma((width,)),
            dma((width,)),
            dma((width,)),
            dma((width,)),
            dma((width,)),
            dma((width,)),
        ],
        compiler_params=pltpu.CompilerParams(
            collective_id=0, has_side_effects=True, vmem_limit_bytes=48 << 20
        ),
        name="smc_round",
    )(
        block_choice,
        tile_slot,
        inverse,
        positions,
        ancestors.reshape(1, particles),
        design,
        labels.reshape(blocks_dev, TILE),
        row_section.reshape(blocks_dev, TILE),
    )
    return advanced, mean.reshape(particles)


def solution(mesh):
    return jax.shard_map(
        shards,
        mesh=mesh,
        in_specs=(P("dom", "dp"), P("dom"), P(), P("dp", None), P("dp", None), P("dp"), P("dp")),
        out_specs=(P("dom", "dp"), P("dom")),
        check_vma=False,
    )
```

time: 150 us -> 62.3 us (0.42)
  Pallas kernels: 0 us -> 52.5 us
  blocking collectives: 48.7 us -> 0 us
  waiting for transfers between devices: 36.2 us -> 0 us
  other arithmetic: 16.3 us -> 0.73 us
  between operations: 14.9 us -> 0.65 us
  matrix products: 12.3 us -> 0 us
  starting transfers between devices: 9.73 us -> 0 us
  local copies, waits for them, and re-layouts: 11.5 us -> 8.04 us
    pallas_call x0 -> x1, Pallas kernels: none -> 52.5 us  [shards(): pl.pallas_call(functools.partial(round_kernel, groups, width), out_shape=...]
    psum x1 -> x0, blocking collectives: 31.5 us -> none  [shards(): totals, counted = lax.psum((totals, counted), 'dp')]
    all_gather x1 -> x0, waiting for transfers between devices: 22.6 us -> none  [shards(): lineage = lax.all_gather(positions, 'dom', axis=0, tiled=True)]
    all_to_all x1 -> x0, blocking collectives: 17.2 us -> none  [shards(): lax.all_to_all(outgoing, 'dp', split_axis=0, concat_axis=0, tiled=True)]
    all_to_all x2 -> x0, waiting for transfers between devices: 12.9 us -> none  [spread_blocks(): lax.all_to_all(outgoing, 'dp', split_axis=1, concat_axis=1, tiled=True)]
    dot_general x3 -> x0, matrix products: 12.3 us -> none  [the longest x1 7.63 us: shards(): jnp.einsum('bpi,bikc->bkpc', residual, design_tiles, preferred_element_ty...]
    all_to_all x2 -> x0, starting transfers between devices: 9.7 us -> none  [spread_blocks(): lax.all_to_all(outgoing, 'dp', split_axis=1, concat_axis=1, tiled=True)]
    scatter-add x1 -> x0, other arithmetic: 9.64 us -> none  [shards(): jax.ops.segment_sum(flat_terms, tile_slot.reshape(-1), num_segments=data_...]
  transfers between devices with their start and end apart: 3 -> 0, of which waited for: 3 -> 0; matrix products, arithmetic and copies ran while one was open for 7% -> 0% of each run, Pallas kernels for 0% -> 0%
where the time goes in v1:
time: 62.3 us; the launch traced here: 61.9 us
  Pallas kernels  52.5 us (84%)
  local copies, waits for them, and re-layouts  8.04 us (13%)
  other arithmetic  0.73 us (1%)
  between operations  0.65 us (1%)
    pallas_call x1, Pallas kernels, shards(): pl.pallas_call(functools.partial(round_kernel, groups, width), out_shape=...  52.5 us
    unnamed x15, local copies, waits for them, and re-layouts  8.04 us

profile of v1, /device:TPU:0, one launch (start us, length us, event | category | flops | bytes accessed | tf_op | source)
XLA Modules:
  0.0 61.9 jit_solution(1242433153403364803)
XLA Ops:
  0.6 0.7 %select_reduce_fusion.inverse = s32[16,16]{1,0:T(8,128)S(1)} fusion(s32[16,8]{0,1:T(8,128)S(1)} %multiply_add_fusion, s32[16,8]{0,1:T(8,128)} %param.10), kind=kLoop, calls=%fused_computation | loop fusion | flops 5888 | bytes 2048 | tf_op jit(solution)/shard_map/reduce_min | solution.py:291
  1.4 0.8 %copy.11.slots = s32[16,8]{1,0:T(8,128)S(1)} copy(s32[16,8]{0,1:T(8,128)} %param.10) | data formatting | bytes 1024 | tf_op args[3]
  2.1 0.0 copy-start
  2.1 2.2 %copy-done = bf16[2048,1024]{1,0:T(8,128)(2,1)S(1)} copy-done((bf16[2048,1024]{1,0:T(8,128)(2,1)S(1)}, bf16[2048,1024]{1,0:T(8,128)(2,1)}, u32[]{:S(2)}) %copy-start) | copy-done | bytes 4194328
  4.3 0.0 copy-start.1
  4.3 1.0 %copy-done.1 = f32[64,2048]{1,0:T(8,128)S(1)} copy-done((f32[64,2048]{1,0:T(8,128)S(1)}, f32[64,2048]{1,0:T(8,128)}, u32[]{:S(2)}) %copy-start.1) | copy-done | bytes 524312
  5.4 0.0 copy-start.2
  5.4 0.7 %copy-done.2 = s32[16,16]{1,0:T(8,128)S(1)} copy-done((s32[16,16]{1,0:T(8,128)S(1)}, s32[16,16]{1,0:T(8,128)}, u32[]{:S(2)}) %copy-start.2) | copy-done | bytes 1048
  6.1 0.0 copy-start.3
  6.1 0.7 %copy-done.3 = s32[2048]{0:T(1024)S(1)} copy-done((s32[2048]{0:T(1024)S(1)}, s32[2048]{0:T(1024)}, u32[]{:S(2)}) %copy-start.3) | copy-done | bytes 8216
  6.8 0.0 copy-start.4
  6.8 0.7 %copy-done.4 = s32[2048]{0:T(1024)S(1)} copy-done((s32[2048]{0:T(1024)S(1)}, s32[2048]{0:T(1024)}, u32[]{:S(2)}) %copy-start.4) | copy-done | bytes 8216
  7.4 0.0 copy-start.5
  7.5 0.7 %copy-done.5 = s32[64]{0:T(128)S(1)} copy-done((s32[64]{0:T(128)S(1)}, s32[64]{0:T(128)}, u32[]{:S(2)}) %copy-start.5) | copy-done | bytes 280
  8.1 52.5 %smc_round.1 = (f32[64,2048]{1,0:T(8,128)S(1)}, f32[1,64]{1,0:T(1,128)S(1)}) custom-call(s32[16,16]{1,0:T(8,128)S(1)} %copy-done.2, s32[16,8]{1,0:T(8,128)S(1)} %copy.11.slots, s32[16,16]{1,0:T(8,128)S(1)} %select_reduce_fusion.inverse, f32[64,2048]{1,0:T(8,128)S(1)} %copy-done.1, s32[1,64]{1,0:T(1,128)S(1)} %bitcast.6, bf16[2048,1024]{1,0:T(8,128)(2,1)S(1)} %copy-done, ...), custom_call_target="tpu_custom_call" | custom-call | tf_op jit(solution)/shard_map/smc_round/pallas_call | solution.py:297
  60.6 0.8 %copy.14 = f32[64,2048]{1,0:T(8,128)} copy(f32[64,2048]{1,0:T(8,128)S(1)} %get-tuple-element.8) | data formatting | bytes 1048576
  61.4 0.5 copy.15
  (1 shorter events, 0.0 us)
Async XLA Ops:
  2.1 2.2 %copy-start = (bf16[2048,1024]{1,0:T(8,128)(2,1)S(1)}, bf16[2048,1024]{1,0:T(8,128)(2,1)}, u32[]{:S(2)}) copy-start(bf16[2048,1024]{1,0:T(8,128)(2,1)} %design_hbm.1) | copy-start | bytes 12582916
  4.3 1.0 %copy-start.1 = (f32[64,2048]{1,0:T(8,128)S(1)}, f32[64,2048]{1,0:T(8,128)}, u32[]{:S(2)}) copy-start(f32[64,2048]{1,0:T(8,128)} %positions.1) | copy-start | bytes 1572868
  5.4 0.7 %copy-start.2 = (s32[16,16]{1,0:T(8,128)S(1)}, s32[16,16]{1,0:T(8,128)}, u32[]{:S(2)}) copy-start(s32[16,16]{1,0:T(8,128)} %choice.1) | copy-start | bytes 3076
  6.1 0.7 %copy-start.3 = (s32[2048]{0:T(1024)S(1)}, s32[2048]{0:T(1024)}, u32[]{:S(2)}) copy-start(s32[2048]{0:T(1024)} %param.12) | copy-start | bytes 24580
  6.8 0.7 %copy-start.4 = (s32[2048]{0:T(1024)S(1)}, s32[2048]{0:T(1024)}, u32[]{:S(2)}) copy-start(s32[2048]{0:T(1024)} %param.13) | copy-start | bytes 24580
  7.4 0.7 %copy-start.5 = (s32[64]{0:T(128)S(1)}, s32[64]{0:T(128)}, u32[]{:S(2)}) copy-start(s32[64]{0:T(128)} %param.8) | copy-start | bytes 772

commit v2 on v1

--- a/solution.py
+++ b/solution.py
@@ -11,6 +11,8 @@
 CURRENT = 2
 STEP_SIZE = 1.0
 PRIOR_PRECISION = 0.05
+ARRIVALS = 4
+TERM = jnp.float32
 MESH = pl.DeviceIdType.MESH
 F32, BF16 = jnp.float32, jnp.bfloat16
 
@@ -18,16 +20,26 @@
 def round_kernel(
     groups,
     width,
+    choice_in,
+    slots_in,
+    positions_in,
+    ancestors_in,
+    design_in,
+    labels_in,
+    sections_in,
+    advanced_out,
+    mean_out,
     choice,
     slots,
+    slots_wide,
+    inverse_wide,
     inverse,
     positions,
     ancestors,
-    design_hbm,
     labels,
     sections,
     advanced,
-    mean_out,
+    gradient,
     design,
     narrow,
     picked,
@@ -43,7 +55,9 @@
     fetched_new,
     totals_own,
     totals_all,
-    design_sem,
+    load_sem,
+    inverse_sem,
+    store_sem,
     dom_send,
     dom_recv,
     pos_send,
@@ -60,7 +74,24 @@
     me, group = lax.axis_index("dp"), lax.axis_index("dom")
     particles = positions.shape[0]
     blocks_owned = positions.shape[1] // TILE
-    blocks_dev, per_block = slots.shape
+    per_block, blocks_dev = slots.shape
+    loads = [
+        pltpu.make_async_copy(source, target, load_sem.at[number])
+        for number, (source, target) in enumerate(
+            (
+                (positions_in, positions),
+                (choice_in, choice),
+                (slots_in, slots_wide),
+                (ancestors_in, ancestors),
+                (slots_in, slots),
+                (labels_in, labels),
+                (sections_in, sections),
+                (design_in, design),
+            )
+        )
+    ]
+    for load in loads:
+        load.start()
 
     def to_dp(source, target, sends, receives, device):
         return pltpu.make_async_remote_copy(
@@ -99,9 +130,8 @@
         pl.semaphore_signal(
             barrier, inc=1, device_id=(lax.rem(group + offset, groups), me), device_id_type=MESH
         )
-    design_copy = pltpu.make_async_copy(design_hbm, design, design_sem)
-    design_copy.start()
-
+    for load in loads[:4]:
+        load.wait()
     for block in range(blocks_owned):
         narrow[block] = positions[:, block * TILE : (block + 1) * TILE].astype(BF16)
 
@@ -114,6 +144,15 @@
     lax.fori_loop(0, width, pick, 0)
     origin = lax.broadcasted_iota(jnp.int32, (groups * particles, particles), 0)
     hot = (origin == ancestors[...]).astype(F32).T.astype(BF16)
+    tiles_dev = blocks_dev * per_block
+    owner = lax.broadcasted_iota(jnp.int32, (width, blocks_dev), 0)
+    first = lax.broadcasted_iota(jnp.int32, (width, blocks_dev), 1) * per_block
+    found = jnp.full((width, blocks_dev), tiles_dev, jnp.int32)
+    for place in range(per_block):
+        found = jnp.where(slots_wide[place : place + 1, :] == owner, first + place, found)
+    inverse_wide[...] = found
+    inverse_copy = pltpu.make_async_copy(inverse_wide, inverse, inverse_sem)
+    inverse_copy.start()
     pl.semaphore_wait(barrier, width + groups - 2)
 
     def dom_copy(device, offset, incoming_side):
@@ -161,13 +200,15 @@
 
     others(send_resampled)
     fetched[me] = resample(me)
-    terms[blocks_dev * per_block] = jnp.zeros((particles, TILE), F32)
-    design_copy.wait()
+    terms[tiles_dev] = jnp.zeros((particles, TILE), F32)
+    for load in loads[4:]:
+        load.wait()
+    inverse_copy.wait()
     others(lambda device: from_dp(outgoing.at[device], fetched, out_send, out_recv, device).wait_recv())
 
     def logits_of(source, row_block):
         weights = jnp.concatenate(
-            [source[slots[row_block, place]] for place in range(per_block)], axis=1
+            [source[slots[place, row_block]] for place in range(per_block)], axis=1
         )
         tiles = design[pl.ds(pl.multiple_of(row_block * TILE, TILE), TILE), :]
         logits = lax.dot_general(
@@ -194,11 +235,14 @@
         return total
 
     def send_sum(device):
-        sums[device] = summed(device)
+        sums[device] = summed(device).astype(sums.dtype)
         to_dp(sums.at[device], incoming, grad_send, grad_recv, device).start()
 
     others(send_sum)
-    incoming[me] = summed(me)
+    own = summed(me)
+    own_choice = choice[me, me]
+    for block in range(blocks_owned):
+        gradient[block] = (own_choice == block).astype(F32) * own
 
     lineage[group] = positions[...]
     for offset in range(1, groups):
@@ -212,14 +256,21 @@
             hot, low, preferred_element_type=F32
         )
 
-    others(lambda device: from_dp(sums.at[device], incoming, grad_send, grad_recv, device).wait_recv())
+    for start in range(1, width, ARRIVALS):
+        devices = [
+            lax.rem(me + offset, width) for offset in range(start, min(start + ARRIVALS, width))
+        ]
+        for device in devices:
+            from_dp(sums.at[device], incoming, grad_send, grad_recv, device).wait_recv()
+        arrived = [(choice[device, me], incoming[device].astype(F32)) for device in devices]
+        for block in range(blocks_owned):
+            total = gradient[block]
+            for chosen, value in arrived:
+                total = total + (chosen == block).astype(F32) * value
+            gradient[block] = total
     for block in range(blocks_owned):
-        gradient = jnp.zeros((particles, TILE), F32)
-        for device in range(width):
-            mine = (choice[device, me] == block).astype(F32)
-            gradient = gradient + mine * incoming[device]
         kept = resampled[block]
-        moved = kept + STEP_SIZE * (gradient - PRIOR_PRECISION * kept)
+        moved = kept + STEP_SIZE * (gradient[block] - PRIOR_PRECISION * kept)
         advanced[:, block * TILE : (block + 1) * TILE] = moved
         narrow[block] = moved.astype(BF16)
 
@@ -228,6 +279,8 @@
         to_dp(outgoing_new.at[device], fetched_new, new_send, new_recv, device).start()
 
     others(send_new)
+    store = pltpu.make_async_copy(advanced, advanced_out, store_sem)
+    store.start()
     fetched_new[me] = narrow[choice[me, me]]
     others(
         lambda device: from_dp(
@@ -269,6 +322,7 @@
         to_dp(totals_own, totals_all, tot_send, tot_recv, device).wait_send()
 
     others(wait_sends)
+    store.wait()
 
     def wait_dom(device, carry):
         for offset in range(1, groups):
@@ -286,11 +340,8 @@
     blocks_owned = features // TILE
     blocks_dev, per_block = tile_slot.shape
     tiles = blocks_dev * per_block
-    numbers = jnp.arange(tiles, dtype=jnp.int32).reshape(1, blocks_dev, per_block)
-    owners = jnp.arange(width, dtype=jnp.int32)[:, None, None]
-    inverse = jnp.min(jnp.where(tile_slot[None] == owners, numbers, tiles), axis=2)
-
-    smem = pl.BlockSpec(memory_space=pltpu.SMEM)
+
+    hbm = pl.BlockSpec(memory_space=pl.ANY)
     vmem = pl.BlockSpec(memory_space=pltpu.VMEM)
     block = (particles, TILE)
     dma = pltpu.SemaphoreType.DMA
@@ -300,9 +351,20 @@
             jax.ShapeDtypeStruct((particles, features), F32),
             jax.ShapeDtypeStruct((1, particles), F32),
         ),
-        in_specs=[smem, smem, smem, vmem, vmem, pl.BlockSpec(memory_space=pl.ANY), vmem, vmem],
-        out_specs=(vmem, vmem),
+        in_specs=[hbm] * 7,
+        out_specs=(hbm, vmem),
         scratch_shapes=[
+            pltpu.SMEM((width, width), jnp.int32),
+            pltpu.SMEM((per_block, blocks_dev), jnp.int32),
+            pltpu.VMEM((per_block, blocks_dev), jnp.int32),
+            pltpu.VMEM((width, blocks_dev), jnp.int32),
+            pltpu.SMEM((width, blocks_dev), jnp.int32),
+            pltpu.VMEM((particles, features), F32),
+            pltpu.VMEM((1, particles), jnp.int32),
+            pltpu.VMEM((blocks_dev, TILE), jnp.int32),
+            pltpu.VMEM((blocks_dev, TILE), jnp.int32),
+            pltpu.VMEM((particles, features), F32),
+            pltpu.VMEM((blocks_owned, *block), F32),
             pltpu.VMEM(design.shape, BF16),
             pltpu.VMEM((blocks_owned, *block), BF16),
             pltpu.VMEM((width, *block), BF16),
@@ -312,12 +374,14 @@
             pltpu.VMEM((width, *block), BF16),
             pltpu.VMEM((width, *block), BF16),
             pltpu.VMEM((tiles + 1, *block), F32),
-            pltpu.VMEM((width, *block), F32),
-            pltpu.VMEM((width, *block), F32),
+            pltpu.VMEM((width, *block), TERM),
+            pltpu.VMEM((width, *block), TERM),
             pltpu.VMEM((width, *block), BF16),
             pltpu.VMEM((width, *block), BF16),
             pltpu.VMEM((8, 2 * particles), F32),
             pltpu.VMEM((width, 8, 2 * particles), F32),
+            dma((8,)),
+            dma,
             dma,
             dma((max(groups - 1, 1), width)),
             dma((max(groups - 1, 1), width)),
@@ -333,13 +397,12 @@
             dma((width,)),
         ],
         compiler_params=pltpu.CompilerParams(
-            collective_id=0, has_side_effects=True, vmem_limit_bytes=48 << 20
+            collective_id=0, has_side_effects=True, vmem_limit_bytes=60 << 20
         ),
         name="smc_round",
     )(
         block_choice,
-        tile_slot,
-        inverse,
+        tile_slot.T,
         positions,
         ancestors.reshape(1, particles),
         design,

time: 62.3 us -> 55.8 us (0.90)
  local copies, waits for them, and re-layouts: 8.04 us -> 2.98 us
  other arithmetic: 0.73 us -> 0 us
    unnamed x15 -> x2, local copies, waits for them, and re-layouts: 8.04 us -> 2.98 us
    reduce_min x1 -> x0, other arithmetic: 0.72 us -> none  [shards(): jnp.min(jnp.where(tile_slot[None] == owners, numbers, tiles), axis=2)]
where the time goes in v2:
time: 55.8 us; the launch traced here: 55.6 us
  Pallas kernels  52 us (93%)
  local copies, waits for them, and re-layouts  2.98 us (5%)
  between operations  0.64 us (1%)
    pallas_call x1, Pallas kernels, shards(): pl.pallas_call(functools.partial(round_kernel, groups, width), out_shape=...  52 us
    unnamed x2, local copies, waits for them, and re-layouts  2.98 us

profile of v2, /device:TPU:0, one launch (start us, length us, event | category | flops | bytes accessed | tf_op | source)
XLA Modules:
  0.0 55.6 jit_solution(11905607393495088536)
XLA Ops:
  0.6 52.0 %smc_round.1 = (f32[64,2048]{1,0:T(8,128)}, f32[1,64]{1,0:T(1,128)}) custom-call(s32[16,16]{1,0:T(8,128)} %choice_in.1, s32[8,16]{1,0:T(8,128)} %bitcast.7, f32[64,2048]{1,0:T(8,128)} %positions_in.1, s32[1,64]{1,0:T(1,128)} %bitcast.8, bf16[2048,1024]{1,0:T(8,128)(2,1)} %design_in.1, s32[16,128]{1,0:T(8,128)} %bitcast.5, s32[16,128]{1,0:T(8,128)} %bitcast.6), custom_call_target="tpu_custom_call" | custom-call | tf_op jit(solution)/shard_map/smc_round/pallas_call | solution.py:348
  52.6 1.9 %copy.11 = f32[64,2048]{1,0:T(8,128)} copy(f32[64,2048]{1,0:T(8,128)} %get-tuple-element.8) | data formatting | bytes 1048576
  54.5 1.1 %copy.12 = f32[64]{0:T(128)} copy(f32[64]{0:T(128)} %bitcast.9) | data formatting | bytes 512

commit v3 on v2

--- a/solution.py
+++ b/solution.py
@@ -12,7 +12,8 @@
 STEP_SIZE = 1.0
 PRIOR_PRECISION = 0.05
 ARRIVALS = 4
-TERM = jnp.float32
+LEVELS = 32767.0
+TINY = 1e-30
 MESH = pl.DeviceIdType.MESH
 F32, BF16 = jnp.float32, jnp.bfloat16
 
@@ -51,6 +52,8 @@
     terms,
     sums,
     incoming,
+    peaks,
+    peaks_in,
     outgoing_new,
     fetched_new,
     totals_own,
@@ -66,6 +69,8 @@
     out_recv,
     grad_send,
     grad_recv,
+    peak_send,
+    peak_recv,
     new_send,
     new_recv,
     tot_send,
@@ -235,7 +240,12 @@
         return total
 
     def send_sum(device):
-        sums[device] = summed(device).astype(sums.dtype)
+        total = summed(device)
+        peak = jnp.max(jnp.abs(total), axis=0, keepdims=True)
+        peaks[device] = peak
+        to_dp(peaks.at[device], peaks_in, peak_send, peak_recv, device).start()
+        coded = jnp.round(total * (LEVELS / jnp.maximum(peak, TINY)))
+        sums[device] = coded.astype(jnp.int32).astype(jnp.int16)
         to_dp(sums.at[device], incoming, grad_send, grad_recv, device).start()
 
     others(send_sum)
@@ -261,8 +271,16 @@
             lax.rem(me + offset, width) for offset in range(start, min(start + ARRIVALS, width))
         ]
         for device in devices:
+            from_dp(peaks.at[device], peaks_in, peak_send, peak_recv, device).wait_recv()
             from_dp(sums.at[device], incoming, grad_send, grad_recv, device).wait_recv()
-        arrived = [(choice[device, me], incoming[device].astype(F32)) for device in devices]
+        arrived = [
+            (
+                choice[device, me],
+                incoming[device].astype(jnp.int32).astype(F32)
+                * (jnp.maximum(peaks_in[device], TINY) * (1.0 / LEVELS)),
+            )
+            for device in devices
+        ]
         for block in range(blocks_owned):
             total = gradient[block]
             for chosen, value in arrived:
@@ -318,6 +336,7 @@
     def wait_sends(device):
         to_dp(outgoing.at[device], fetched, out_send, out_recv, device).wait_send()
         to_dp(sums.at[device], incoming, grad_send, grad_recv, device).wait_send()
+        to_dp(peaks.at[device], peaks_in, peak_send, peak_recv, device).wait_send()
         to_dp(outgoing_new.at[device], fetched_new, new_send, new_recv, device).wait_send()
         to_dp(totals_own, totals_all, tot_send, tot_recv, device).wait_send()
 
@@ -374,8 +393,10 @@
             pltpu.VMEM((width, *block), BF16),
             pltpu.VMEM((width, *block), BF16),
             pltpu.VMEM((tiles + 1, *block), F32),
-            pltpu.VMEM((width, *block), TERM),
-            pltpu.VMEM((width, *block), TERM),
+            pltpu.VMEM((width, *block), jnp.int16),
+            pltpu.VMEM((width, *block), jnp.int16),
+            pltpu.VMEM((width, 1, TILE), F32),
+            pltpu.VMEM((width, 1, TILE), F32),
             pltpu.VMEM((width, *block), BF16),
             pltpu.VMEM((width, *block), BF16),
             pltpu.VMEM((8, 2 * particles), F32),
@@ -387,6 +408,8 @@
             dma((max(groups - 1, 1), width)),
             dma((max(groups - 1, 1),)),
             dma((max(groups - 1, 1),)),
+            dma((width,)),
+            dma((width,)),
             dma((width,)),
             dma((width,)),
             dma((width,)),

time: 55.8 us -> 51.3 us (0.919)
  Pallas kernels: 52 us -> 47.5 us
    pallas_call x1, Pallas kernels: 52 us -> 47.5 us  [shards(): pl.pallas_call(functools.partial(round_kernel, groups, width), out_shape=...]
where the time goes in v3:
time: 51.3 us; the launch traced here: 51.1 us
  Pallas kernels  47.5 us (93%)
  local copies, waits for them, and re-layouts  2.98 us (6%)
  between operations  0.64 us (1%)
    pallas_call x1, Pallas kernels, shards(): pl.pallas_call(functools.partial(round_kernel, groups, width), out_shape=...  47.5 us
    unnamed x2, local copies, waits for them, and re-layouts  2.98 us

profile of v3, /device:TPU:0, one launch (start us, length us, event | category | flops | bytes accessed | tf_op | source)
XLA Modules:
  0.0 51.1 jit_solution(8463630238075108011)
XLA Ops:
  0.6 47.5 %smc_round.1 = (f32[64,2048]{1,0:T(8,128)}, f32[1,64]{1,0:T(1,128)}) custom-call(s32[16,16]{1,0:T(8,128)} %choice_in.1, s32[8,16]{1,0:T(8,128)} %bitcast.7, f32[64,2048]{1,0:T(8,128)} %positions_in.1, s32[1,64]{1,0:T(1,128)} %bitcast.8, bf16[2048,1024]{1,0:T(8,128)(2,1)} %design_in.1, s32[16,128]{1,0:T(8,128)} %bitcast.5, s32[16,128]{1,0:T(8,128)} %bitcast.6), custom_call_target="tpu_custom_call" | custom-call | tf_op jit(solution)/shard_map/smc_round/pallas_call | solution.py:367
  48.1 1.9 %copy.11 = f32[64,2048]{1,0:T(8,128)} copy(f32[64,2048]{1,0:T(8,128)} %get-tuple-element.8) | data formatting | bytes 1048576
  50.0 1.1 %copy.12 = f32[64]{0:T(128)} copy(f32[64]{0:T(128)} %bitcast.9) | data formatting | bytes 512

commit v4 on v3

--- a/solution.py
+++ b/solution.py
@@ -16,6 +16,11 @@
 TINY = 1e-30
 MESH = pl.DeviceIdType.MESH
 F32, BF16 = jnp.float32, jnp.bfloat16
+
+
+def far_first(turn, width):
+    odd = turn % 2
+    return width // 2 + odd * ((turn + 1) // 2) - (1 - odd) * (turn // 2) if width % 2 == 0 else turn + 1
 
 
 def round_kernel(
@@ -119,11 +124,11 @@
         )
 
     def others(body):
-        def step(offset, carry):
-            body(lax.rem(me + offset, width))
+        def step(turn, carry):
+            body(lax.rem(me + far_first(turn, width), width))
             return carry
 
-        lax.fori_loop(1, width, step, 0)
+        lax.fori_loop(0, width - 1, step, 0)
 
     barrier = pltpu.get_barrier_semaphore()
 
@@ -266,9 +271,10 @@
             hot, low, preferred_element_type=F32
         )
 
-    for start in range(1, width, ARRIVALS):
+    for start in range(0, width - 1, ARRIVALS):
         devices = [
-            lax.rem(me + offset, width) for offset in range(start, min(start + ARRIVALS, width))
+            lax.rem(me + far_first(turn, width), width)
+            for turn in range(start, min(start + ARRIVALS, width - 1))
         ]
         for device in devices:
             from_dp(peaks.at[device], peaks_in, peak_send, peak_recv, device).wait_recv()

time: 51.3 us -> 52.3 us (1.019)
  Pallas kernels: 47.5 us -> 48.5 us
    pallas_call x1, Pallas kernels: 47.5 us -> 48.5 us  [shards(): pl.pallas_call(functools.partial(round_kernel, groups, width), out_shape=...]
where the time goes in v4:
time: 52.3 us; the launch traced here: 52.2 us
  Pallas kernels  48.5 us (93%)
  local copies, waits for them, and re-layouts  2.98 us (6%)
  between operations  0.64 us (1%)
    pallas_call x1, Pallas kernels, shards(): pl.pallas_call(functools.partial(round_kernel, groups, width), out_shape=...  48.5 us
    unnamed x2, local copies, waits for them, and re-layouts  2.98 us

profile of v4, /device:TPU:0, one launch (start us, length us, event | category | flops | bytes accessed | tf_op | source)
XLA Modules:
  0.0 52.2 jit_solution(11602805377745457259)
XLA Ops:
  0.6 48.5 %smc_round.1 = (f32[64,2048]{1,0:T(8,128)}, f32[1,64]{1,0:T(1,128)}) custom-call(s32[16,16]{1,0:T(8,128)} %choice_in.1, s32[8,16]{1,0:T(8,128)} %bitcast.7, f32[64,2048]{1,0:T(8,128)} %positions_in.1, s32[1,64]{1,0:T(1,128)} %bitcast.8, bf16[2048,1024]{1,0:T(8,128)(2,1)} %design_in.1, s32[16,128]{1,0:T(8,128)} %bitcast.5, s32[16,128]{1,0:T(8,128)} %bitcast.6), custom_call_target="tpu_custom_call" | custom-call | tf_op jit(solution)/shard_map/smc_round/pallas_call | solution.py:373
  49.2 1.9 %copy.11 = f32[64,2048]{1,0:T(8,128)} copy(f32[64,2048]{1,0:T(8,128)} %get-tuple-element.8) | data formatting | bytes 1048576
  51.1 1.1 %copy.12 = f32[64]{0:T(128)} copy(f32[64]{0:T(128)} %bitcast.9) | data formatting | bytes 512

commit v5 on v3

--- a/solution.py
+++ b/solution.py
@@ -49,6 +49,7 @@
     resampled,
     outgoing,
     fetched,
+    residual,
     terms,
     sums,
     incoming,
@@ -190,8 +191,6 @@
 
     others(send_picked)
     send_picked(me)
-    for offset in range(1, groups):
-        position_copy(offset, False).start()
 
     def resample(device):
         for offset in range(1, groups):
@@ -205,6 +204,8 @@
 
     others(send_resampled)
     fetched[me] = resample(me)
+    for offset in range(1, groups):
+        position_copy(offset, False).start()
     terms[tiles_dev] = jnp.zeros((particles, TILE), F32)
     for load in loads[4:]:
         load.wait()
@@ -221,17 +222,25 @@
         )
         target = labels[pl.ds(row_block, 1), :].astype(F32)
         section = sections[pl.ds(row_block, 1), :]
-        return tiles, logits, target, section
+        return logits, target, section
+
+    def residuals(row_block, carry):
+        logits, target, section = logits_of(fetched, row_block)
+        residual[row_block] = jnp.where(
+            section <= CURRENT, target - jax.nn.sigmoid(logits), 0.0
+        ).astype(BF16)
+        return carry
+
+    lax.fori_loop(0, blocks_dev, residuals, 0, unroll=8)
 
     def gradient_terms(row_block, carry):
-        tiles, logits, target, section = logits_of(fetched, row_block)
-        residual = jnp.where(section <= CURRENT, target - jax.nn.sigmoid(logits), 0.0).astype(BF16)
-        product = jnp.dot(residual, tiles, preferred_element_type=F32)
+        tiles = design[pl.ds(pl.multiple_of(row_block * TILE, TILE), TILE), :]
+        product = jnp.dot(residual[row_block], tiles, preferred_element_type=F32)
         for place in range(per_block):
             terms[row_block * per_block + place] = product[:, place * TILE : (place + 1) * TILE]
         return carry
 
-    lax.fori_loop(0, blocks_dev, gradient_terms, 0, unroll=4)
+    lax.fori_loop(0, blocks_dev, gradient_terms, 0, unroll=8)
 
     def summed(device):
         total = terms[inverse[device, 0]]
@@ -308,7 +317,7 @@
 
     def likelihood(row_block, carry):
         total, counted = carry
-        _, logits, target, section = logits_of(fetched_new, row_block)
+        logits, target, section = logits_of(fetched_new, row_block)
         chosen = section == CURRENT + 1
         softplus = jnp.maximum(logits, 0.0) + jnp.log(1.0 + jnp.exp(-jnp.abs(logits)))
         return (
@@ -321,7 +330,7 @@
         blocks_dev,
         likelihood,
         (jnp.zeros((particles, TILE), F32), jnp.zeros((1, TILE), F32)),
-        unroll=4,
+        unroll=8,
     )
     both = jnp.concatenate([total, jnp.broadcast_to(counted, (particles, TILE))], axis=0)
     row = jnp.sum(both.T, axis=0, keepdims=True)
@@ -392,6 +401,7 @@
             pltpu.VMEM((blocks_owned, *block), F32),
             pltpu.VMEM((width, *block), BF16),
             pltpu.VMEM((width, *block), BF16),
+            pltpu.VMEM((blocks_dev, *block), BF16),
             pltpu.VMEM((tiles + 1, *block), F32),
             pltpu.VMEM((width, *block), jnp.int16),
             pltpu.VMEM((width, *block), jnp.int16),

time: 51.3 us -> 47.9 us (0.934)
  Pallas kernels: 47.5 us -> 44.1 us
    pallas_call x1, Pallas kernels: 47.5 us -> 44.1 us  [shards(): pl.pallas_call(functools.partial(round_kernel, groups, width), out_shape=...]
where the time goes in v5:
time: 47.9 us; the launch traced here: 47.7 us
  Pallas kernels  44.1 us (92%)
  local copies, waits for them, and re-layouts  2.98 us (6%)
  between operations  0.64 us (1%)
    pallas_call x1, Pallas kernels, shards(): pl.pallas_call(functools.partial(round_kernel, groups, width), out_shape=...  44.1 us
    unnamed x2, local copies, waits for them, and re-layouts  2.98 us

profile of v5, /device:TPU:0, one launch (start us, length us, event | category | flops | bytes accessed | tf_op | source)
XLA Modules:
  0.0 47.7 jit_solution(17803429490163373619)
XLA Ops:
  0.6 44.1 %smc_round.1 = (f32[64,2048]{1,0:T(8,128)}, f32[1,64]{1,0:T(1,128)}) custom-call(s32[16,16]{1,0:T(8,128)} %choice_in.1, s32[8,16]{1,0:T(8,128)} %bitcast.7, f32[64,2048]{1,0:T(8,128)} %positions_in.1, s32[1,64]{1,0:T(1,128)} %bitcast.8, bf16[2048,1024]{1,0:T(8,128)(2,1)} %design_in.1, s32[16,128]{1,0:T(8,128)} %bitcast.5, s32[16,128]{1,0:T(8,128)} %bitcast.6), custom_call_target="tpu_custom_call" | custom-call | tf_op jit(solution)/shard_map/smc_round/pallas_call | solution.py:376
  44.7 1.9 %copy.11 = f32[64,2048]{1,0:T(8,128)} copy(f32[64,2048]{1,0:T(8,128)} %get-tuple-element.8) | data formatting | bytes 1048576
  46.6 1.1 %copy.12 = f32[64]{0:T(128)} copy(f32[64]{0:T(128)} %bitcast.9) | data formatting | bytes 512

commit v6 on v5

--- a/solution.py
+++ b/solution.py
@@ -12,6 +12,7 @@
 STEP_SIZE = 1.0
 PRIOR_PRECISION = 0.05
 ARRIVALS = 4
+GROUP = 3
 LEVELS = 32767.0
 TINY = 1e-30
 MESH = pl.DeviceIdType.MESH
@@ -126,6 +127,15 @@
 
         lax.fori_loop(1, width, step, 0)
 
+    def grouped(body):
+        size = GROUP if (width - 1) % GROUP == 0 else 1
+
+        def step(turn, carry):
+            body([lax.rem(me + 1 + turn * size + place, width) for place in range(size)])
+            return carry
+
+        lax.fori_loop(0, (width - 1) // size, step, 0)
+
     barrier = pltpu.get_barrier_semaphore()
 
     def greet(device):
@@ -192,18 +202,24 @@
     others(send_picked)
     send_picked(me)
 
-    def resample(device):
-        for offset in range(1, groups):
-            dom_copy(device, offset, True).wait_recv()
-        rows = picked_all[:, device].reshape(groups * particles, TILE)
-        return jnp.dot(hot, rows, preferred_element_type=F32).astype(BF16)
-
-    def send_resampled(device):
-        outgoing[device] = resample(device)
-        to_dp(outgoing.at[device], fetched, out_send, out_recv, device).start()
-
-    others(send_resampled)
-    fetched[me] = resample(me)
+    def resample(devices):
+        for device in devices:
+            for offset in range(1, groups):
+                dom_copy(device, offset, True).wait_recv()
+        rows = jnp.concatenate(
+            [picked_all[:, device].reshape(groups * particles, TILE) for device in devices], axis=1
+        )
+        drawn = jnp.dot(hot, rows, preferred_element_type=F32).astype(BF16)
+        return [drawn[:, place * TILE : (place + 1) * TILE] for place in range(len(devices))]
+
+    def send_resampled(devices):
+        for device, value in zip(devices, resample(devices)):
+            outgoing[device] = value
+        for device in devices:
+            to_dp(outgoing.at[device], fetched, out_send, out_recv, device).start()
+
+    grouped(send_resampled)
+    fetched[me] = resample([me])[0]
     for offset in range(1, groups):
         position_copy(offset, False).start()
     terms[tiles_dev] = jnp.zeros((particles, TILE), F32)
@@ -218,8 +234,8 @@
         )
         tiles = design[pl.ds(pl.multiple_of(row_block * TILE, TILE), TILE), :]
         logits = lax.dot_general(
-            weights, tiles, (((1,), (1,)), ((), ())), preferred_element_type=F32
-        )
+            tiles, weights, (((1,), (1,)), ((), ())), preferred_element_type=F32
+        ).T
         target = labels[pl.ds(row_block, 1), :].astype(F32)
         section = sections[pl.ds(row_block, 1), :]
         return logits, target, section
@@ -248,16 +264,18 @@
             total = total + terms[inverse[device, row_block]]
         return total
 
-    def send_sum(device):
-        total = summed(device)
-        peak = jnp.max(jnp.abs(total), axis=0, keepdims=True)
-        peaks[device] = peak
-        to_dp(peaks.at[device], peaks_in, peak_send, peak_recv, device).start()
-        coded = jnp.round(total * (LEVELS / jnp.maximum(peak, TINY)))
-        sums[device] = coded.astype(jnp.int32).astype(jnp.int16)
-        to_dp(sums.at[device], incoming, grad_send, grad_recv, device).start()
-
-    others(send_sum)
+    def send_sums(devices):
+        for device in devices:
+            total = summed(device)
+            peak = jnp.max(jnp.abs(total), axis=0, keepdims=True)
+            peaks[device] = peak
+            coded = jnp.round(total * (LEVELS / jnp.maximum(peak, TINY)))
+            sums[device] = coded.astype(jnp.int32).astype(jnp.int16)
+        for device in devices:
+            to_dp(peaks.at[device], peaks_in, peak_send, peak_recv, device).start()
+            to_dp(sums.at[device], incoming, grad_send, grad_recv, device).start()
+
+    grouped(send_sums)
     own = summed(me)
     own_choice = choice[me, me]
     for block in range(blocks_owned):
@@ -301,11 +319,13 @@
         advanced[:, block * TILE : (block + 1) * TILE] = moved
         narrow[block] = moved.astype(BF16)
 
-    def send_new(device):
-        outgoing_new[device] = narrow[choice[device, me]]
-        to_dp(outgoing_new.at[device], fetched_new, new_send, new_recv, device).start()
-
-    others(send_new)
+    def send_new(devices):
+        for device in devices:
+            outgoing_new[device] = narrow[choice[device, me]]
+        for device in devices:
+            to_dp(outgoing_new.at[device], fetched_new, new_send, new_recv, device).start()
+
+    grouped(send_new)
     store = pltpu.make_async_copy(advanced, advanced_out, store_sem)
     store.start()
     fetched_new[me] = narrow[choice[me, me]]

time: 47.9 us -> 48.1 us (level)
  no operation moved by 1% of the time
where the time goes in v6:
time: 48.1 us; the launch traced here: 48 us
  Pallas kernels  44.3 us (92%)
  local copies, waits for them, and re-layouts  2.98 us (6%)
  between operations  0.64 us (1%)
    pallas_call x1, Pallas kernels, shards(): pl.pallas_call(functools.partial(round_kernel, groups, width), out_shape=...  44.3 us
    unnamed x2, local copies, waits for them, and re-layouts  2.98 us

profile of v6, /device:TPU:0, one launch (start us, length us, event | category | flops | bytes accessed | tf_op | source)
XLA Modules:
  0.0 48.0 jit_solution(9912000505206550273)
XLA Ops:
  0.6 44.3 %smc_round.1 = (f32[64,2048]{1,0:T(8,128)}, f32[1,64]{1,0:T(1,128)}) custom-call(s32[16,16]{1,0:T(8,128)} %choice_in.1, s32[8,16]{1,0:T(8,128)} %bitcast.7, f32[64,2048]{1,0:T(8,128)} %positions_in.1, s32[1,64]{1,0:T(1,128)} %bitcast.8, bf16[2048,1024]{1,0:T(8,128)(2,1)} %design_in.1, s32[16,128]{1,0:T(8,128)} %bitcast.5, s32[16,128]{1,0:T(8,128)} %bitcast.6), custom_call_target="tpu_custom_call" | custom-call | tf_op jit(solution)/shard_map/smc_round/pallas_call | solution.py:396
  45.0 1.9 %copy.11 = f32[64,2048]{1,0:T(8,128)} copy(f32[64,2048]{1,0:T(8,128)} %get-tuple-element.8) | data formatting | bytes 1048576
  46.8 1.1 %copy.12 = f32[64]{0:T(128)} copy(f32[64]{0:T(128)} %bitcast.9) | data formatting | bytes 512

commit v7 on v5

--- a/solution.py
+++ b/solution.py
@@ -45,6 +45,10 @@
     narrow,
     picked,
     picked_all,
+    coded_peak,
+    coded_rows,
+    lineage_peak,
+    lineage_rows,
     lineage,
     resampled,
     outgoing,
@@ -173,17 +177,22 @@
             device_id_type=MESH,
         )
 
-    def position_copy(offset, incoming_side):
+    def position_copies(offset, incoming_side):
         sign = groups - offset if incoming_side else offset
         peer = lax.rem(group + sign, groups)
-        return pltpu.make_async_remote_copy(
-            src_ref=positions,
-            dst_ref=lineage.at[peer if incoming_side else group],
-            send_sem=pos_send.at[offset - 1],
-            recv_sem=pos_recv.at[offset - 1],
-            device_id=(peer, me),
-            device_id_type=MESH,
-        )
+        return [
+            pltpu.make_async_remote_copy(
+                src_ref=source,
+                dst_ref=target.at[peer if incoming_side else group],
+                send_sem=pos_send.at[kind, offset - 1],
+                recv_sem=pos_recv.at[kind, offset - 1],
+                device_id=(peer, me),
+                device_id_type=MESH,
+            )
+            for kind, (source, target) in enumerate(
+                ((coded_peak, lineage_peak), (coded_rows, lineage_rows))
+            )
+        ]
 
     def send_picked(device):
         for offset in range(1, groups):
@@ -204,8 +213,16 @@
 
     others(send_resampled)
     fetched[me] = resample(me)
+    own_peak = jnp.max(jnp.abs(positions[...]), axis=0, keepdims=True)
+    coded_peak[...] = own_peak
+    coded_rows[...] = (
+        jnp.round(positions[...] * (LEVELS / jnp.maximum(own_peak, TINY)))
+        .astype(jnp.int32)
+        .astype(jnp.int16)
+    )
     for offset in range(1, groups):
-        position_copy(offset, False).start()
+        for copy in position_copies(offset, False):
+            copy.start()
     terms[tiles_dev] = jnp.zeros((particles, TILE), F32)
     for load in loads[4:]:
         load.wait()
@@ -265,7 +282,12 @@
 
     lineage[group] = positions[...]
     for offset in range(1, groups):
-        position_copy(offset, True).wait_recv()
+        for copy in position_copies(offset, True):
+            copy.wait_recv()
+        peer = lax.rem(group + groups - offset, groups)
+        lineage[peer] = lineage_rows[peer].astype(jnp.int32).astype(F32) * (
+            jnp.maximum(lineage_peak[peer], TINY) * (1.0 / LEVELS)
+        )
     for block in range(blocks_owned):
         span = slice(block * TILE, (block + 1) * TILE)
         rows = lineage[:, :, span].reshape(groups * particles, TILE)
@@ -359,7 +381,8 @@
 
     lax.fori_loop(0, width, wait_dom, 0)
     for offset in range(1, groups):
-        position_copy(offset, False).wait_send()
+        for copy in position_copies(offset, False):
+            copy.wait_send()
 
 
 def shards(positions, ancestors, block_choice, tile_slot, design, labels, row_section):
@@ -397,6 +420,10 @@
             pltpu.VMEM((blocks_owned, *block), BF16),
             pltpu.VMEM((width, *block), BF16),
             pltpu.VMEM((groups, width, *block), BF16),
+            pltpu.VMEM((1, features), F32),
+            pltpu.VMEM((particles, features), jnp.int16),
+            pltpu.VMEM((groups, 1, features), F32),
+            pltpu.VMEM((groups, particles, features), jnp.int16),
             pltpu.VMEM((groups, particles, features), F32),
             pltpu.VMEM((blocks_owned, *block), F32),
             pltpu.VMEM((width, *block), BF16),
@@ -416,8 +443,8 @@
             dma,
             dma((max(groups - 1, 1), width)),
             dma((max(groups - 1, 1), width)),
-            dma((max(groups - 1, 1),)),
-            dma((max(groups - 1, 1),)),
+            dma((2, max(groups - 1, 1))),
+            dma((2, max(groups - 1, 1))),
             dma((width,)),
             dma((width,)),
             dma((width,)),

time: 47.9 us -> 48 us (level)
  no operation moved by 1% of the time
where the time goes in v7:
time: 48 us; the launch traced here: 47.8 us
  Pallas kernels  44.2 us (92%)
  local copies, waits for them, and re-layouts  2.98 us (6%)
  between operations  0.64 us (1%)
    pallas_call x1, Pallas kernels, shards(): pl.pallas_call(functools.partial(round_kernel, groups, width), out_shape=...  44.2 us
    unnamed x2, local copies, waits for them, and re-layouts  2.98 us

profile of v7, /device:TPU:0, one launch (start us, length us, event | category | flops | bytes accessed | tf_op | source)
XLA Modules:
  0.0 47.8 jit_solution(17446362813131010978)
XLA Ops:
  0.6 44.2 %smc_round.1 = (f32[64,2048]{1,0:T(8,128)}, f32[1,64]{1,0:T(1,128)}) custom-call(s32[16,16]{1,0:T(8,128)} %choice_in.1, s32[8,16]{1,0:T(8,128)} %bitcast.7, f32[64,2048]{1,0:T(8,128)} %positions_in.1, s32[1,64]{1,0:T(1,128)} %bitcast.8, bf16[2048,1024]{1,0:T(8,128)(2,1)} %design_in.1, s32[16,128]{1,0:T(8,128)} %bitcast.5, s32[16,128]{1,0:T(8,128)} %bitcast.6), custom_call_target="tpu_custom_call" | custom-call | tf_op jit(solution)/shard_map/smc_round/pallas_call | solution.py:399
  44.9 1.9 %copy.11 = f32[64,2048]{1,0:T(8,128)} copy(f32[64,2048]{1,0:T(8,128)} %get-tuple-element.8) | data formatting | bytes 1048576
  46.7 1.1 %copy.12 = f32[64]{0:T(128)} copy(f32[64]{0:T(128)} %bitcast.9) | data formatting | bytes 512
